TPU v7x, 512 devices: a whole 4x4x16 slice. The times are simulated.
512 devices in a mesh: ctx: 64 (over z, x), head: 8 (over y, core).
Axes of the slice: x: 4, y: 4, z: 16, core: 2. Of those that a mesh axis runs over, the one named last changes fastest.
Arguments:
- queries: float32 [32768, 2048], P('ctx', 'head'), may hold values from -1024 to 1024
- keys: float32 [32768, 128], P('ctx'), may hold values from -1024 to 1024
- values: float32 [32768, 128], P('ctx'), may hold values from -6 to 6
- cotangent: float32 [32768, 2048], P('ctx', 'head'), may hold values from -384 to 384
- source_ids: int32 [32768], P('ctx'), may hold values from 0 to 63
- source_weights: float32 [64], replicated, may hold values from 0.25 to 4
- q_feature: float32 [16, 128, 128], P('head'), may hold values from -4 to 4
- k_feature: float32 [128, 128], replicated, may hold values from -4 to 4
Outputs:
- grad_queries: float32 [32768, 2048], P('ctx', 'head')
- grad_keys: float32 [32768, 128], P(('ctx', 'head'))
- grad_values: float32 [32768, 128], P(('ctx', 'head'))
- grad_q_feature: float32 [16, 128, 128], P('head')
- grad_k_feature: float32 [128, 128], replicated
All inputs are finite; a program needn't handle non-finite values.
Results may differ from a plain program's by a relative error of at most 0.0015.
Values sent between devices are 32-bit elements; how exact they have to be, the bound alone decides.
A program may use at most 64 MiB of HBM per device.

v0:
```python
import jax
import jax.numpy as jnp
from jax import lax
from jax.sharding import PartitionSpec as P


def entering(value, axis, join, neutral, backward):
    count, mine = (lax.axis_size(axis), lax.axis_index(axis))
    pieces = jax.tree.map(lambda part: lax.all_gather(part, axis), value)
    if backward:
        pieces = jax.tree.map(lambda part: part[::-1], pieces)
        mine = count - 1 - mine
    total = jax.tree.map(
        lambda part, zero: jnp.full_like(part, 0) + jnp.asarray(zero, part.dtype), value, neutral
    )

    def turn(position, total):
        longer = join(total, jax.tree.map(lambda part: part[position], pieces))
        return jax.tree.map(lambda new, old: jnp.where(position < mine, new, old), longer, total)

    return lax.fori_loop(0, count - 1, turn, total)


def matmul(left, right):
    return jnp.dot(left, right, precision=lax.Precision.HIGHEST, preferred_element_type=jnp.float32)


def product(form, left, right):
    return jnp.einsum(
        form, left, right, precision=lax.Precision.HIGHEST, preferred_element_type=jnp.float32
    )


def feature_map(inputs, weight):
    logits = matmul(inputs, weight)
    upper = jax.nn.softmax(logits, axis=-1)
    lower = jax.nn.softmax(-logits, axis=-1)
    return (jnp.concatenate([upper, lower], axis=-1), upper, lower)


def feature_back(inputs, weight, upper, lower, grad_feat):
    half = upper.shape[-1]
    grad_upper = grad_feat[:, :half]
    grad_lower = grad_feat[:, half:]
    grad_logits = upper * (grad_upper - jnp.sum(upper * grad_upper, axis=-1, keepdims=True))
    grad_logits = grad_logits - lower * (
        grad_lower - jnp.sum(lower * grad_lower, axis=-1, keepdims=True)
    )
    return (matmul(grad_logits, weight.T), matmul(inputs.T, grad_logits))


def causal_mask(count):
    row_index = lax.broadcasted_iota(jnp.int32, (count, count), 0)
    col_index = lax.broadcasted_iota(jnp.int32, (count, count), 1)
    return (row_index >= col_index).astype(jnp.float32)


def add_pair(earlier, later):
    return (earlier[0] + later[0], earlier[1] + later[1])


def block_terms(query_c, key_c, value_c, scaled_c, prefix, prefix_tot):
    lower_mask = causal_mask(query_c.shape[1])
    scores = product("ncf,ndf->ncd", query_c, key_c) * lower_mask
    numerator = product("ncd,nde->nce", scores, value_c) + product("ncf,nfe->nce", query_c, prefix)
    normalizer = jnp.sum(scores, axis=2) + product("ncf,nf->nc", query_c, prefix_tot)
    output = numerator / normalizer[..., None]
    grad_numer = scaled_c / normalizer[..., None]
    grad_norm = -jnp.sum(scaled_c * output, axis=2) / normalizer
    grad_scores = (product("nce,nde->ncd", grad_numer, value_c) + grad_norm[..., None]) * lower_mask
    grad_query = (
        product("ncd,ndf->ncf", grad_scores, key_c)
        + product("nce,nfe->ncf", grad_numer, prefix)
        + grad_norm[..., None] * prefix_tot[:, None, :]
    )
    grad_key = product("ncd,ncf->ndf", grad_scores, query_c)
    grad_value = product("ncd,nce->nde", scores, grad_numer)
    carried = product("ncf,nce->nfe", query_c, grad_numer)
    carried_totals = product("nc,ncf->nf", grad_norm, query_c)
    return (grad_query, grad_key, grad_value, carried, carried_totals)


def on_device(queries, keys, values, cotangent, source_ids, source_weights, q_feature, k_feature):
    head_count = q_feature.shape[0]
    width = q_feature.shape[1]
    features = 2 * q_feature.shape[2]
    rows = queries.shape[0]
    piece = min(128, rows)
    pieces = rows // piece
    source_index = lax.broadcasted_iota(jnp.int32, (1, source_weights.shape[0]), 1)
    lookup = (source_ids[:, None] == source_index).astype(jnp.float32)
    weight = jnp.sum(lookup * source_weights[None, :], axis=1)
    key_feat, key_upper, key_lower = feature_map(keys, k_feature)
    key_c = key_feat.reshape(pieces, piece, features)
    value_c = values.reshape(pieces, piece, width)
    piece_state = product("ncf,nce->nfe", key_c, value_c)
    piece_tot = jnp.sum(key_c, axis=1)
    whole_local = (jnp.sum(piece_state, axis=0), jnp.sum(piece_tot, axis=0))
    whole_zero = (jnp.zeros((features, width), jnp.float32), jnp.zeros((features,), jnp.float32))
    earlier, earlier_totals = entering(
        (whole_local[0], whole_local[1]), "ctx", add_pair, whole_zero, False
    )
    prefix = jnp.cumsum(piece_state, axis=0) - piece_state + earlier[None]
    prefix_tot = jnp.cumsum(piece_tot, axis=0) - piece_tot + earlier_totals[None]
    grad_keyfeat = jnp.zeros(key_feat.shape, jnp.float32)
    grad_vals = jnp.zeros(values.shape, jnp.float32)
    piece_carried = jnp.zeros((pieces, features, width), jnp.float32)
    piece_carried_tot = jnp.zeros((pieces, features), jnp.float32)
    query_grads = []
    weight_grads = []
    for head in range(head_count):
        query_head = queries[:, head * width : (head + 1) * width]
        query_feat, query_upper, query_lower = feature_map(query_head, q_feature[head])
        scaled = cotangent[:, head * width : (head + 1) * width] * weight[:, None]
        grad_query, grad_key, grad_value, carried, carried_totals = block_terms(
            query_feat.reshape(pieces, piece, features),
            key_c,
            value_c,
            scaled.reshape(pieces, piece, width),
            prefix,
            prefix_tot,
        )
        grad_head, grad_weight = feature_back(
            query_head,
            q_feature[head],
            query_upper,
            query_lower,
            grad_query.reshape(rows, features),
        )
        query_grads.append(grad_head)
        weight_grads.append(grad_weight)
        grad_keyfeat = grad_keyfeat + grad_key.reshape(rows, features)
        grad_vals = grad_vals + grad_value.reshape(rows, width)
        piece_carried = piece_carried + carried
        piece_carried_tot = piece_carried_tot + carried_totals
    carried_all = jnp.sum(piece_carried, axis=0)
    carried_tot = jnp.sum(piece_carried_tot, axis=0)
    inner_later = carried_all[None] - jnp.cumsum(piece_carried, axis=0)
    inner_tot = carried_tot[None] - jnp.cumsum(piece_carried_tot, axis=0)
    grad_keyfeat = grad_keyfeat + (
        product("nce,nfe->ncf", value_c, inner_later) + inner_tot[:, None, :]
    ).reshape(rows, features)
    grad_vals = grad_vals + product("ncf,nfe->nce", key_c, inner_later).reshape(rows, width)
    later, later_tot = entering((carried_all, carried_tot), "ctx", add_pair, whole_zero, True)
    grad_keyfeat = grad_keyfeat + matmul(values, later.T) + later_tot[None, :]
    grad_vals = grad_vals + matmul(key_feat, later)
    grad_key_part, grad_kweight = feature_back(keys, k_feature, key_upper, key_lower, grad_keyfeat)
    grad_keys, grad_values = (
        lax.psum_scatter(grad_key_part, "head", scatter_dimension=0, tiled=True),
        lax.psum_scatter(grad_vals, "head", scatter_dimension=0, tiled=True),
    )
    grad_qweight = lax.psum(jnp.stack(weight_grads, axis=0), "ctx")
    grad_kweight = lax.psum(grad_kweight, ("ctx", "head"))
    return (
        jnp.concatenate(query_grads, axis=1),
        grad_keys,
        grad_values,
        grad_qweight,
        grad_kweight,
    )


def solution(mesh):
    placed = (
        P("ctx", "head"),
        P("ctx", None),
        P("ctx", None),
        P("ctx", "head"),
        P("ctx"),
        P(),
        P("head", None, None),
        P(),
    )
    return jax.shard_map(
        on_device,
        mesh=mesh,
        in_specs=placed,
        out_specs=(
            P("ctx", "head"),
            P(("ctx", "head"), None),
            P(("ctx", "head"), None),
            P("head", None, None),
            P(),
        ),
        check_vma=False,
    )
```

profile of v0, /device:TPU:2, one launch (start us, length us, event | category | flops | bytes accessed | tf_op | source)
XLA Modules:
  0.0 1215.9 jit_solution(13639607046449780209)
XLA Ops:
  7.2 1.5 fusion.97
  9.8 2.1 fusion.103
  14.9 87.9 %all-gather.4 = f32[64,1,256]{2,1,0:T(1,128)S(1)} all-gather(f32[1,1,256]{2,1,0:T(1,128)S(1)} %bitcast.226), channel_id=3, replica_groups=mesh['ctx'=64,'head'=8] {'ctx'}, dimensions={0}, use_global_device_ids=true | all-gather | bytes 66560 | tf_op jit(solution)/shard_map/all_gather | solution.py:9
  106.6 1.8 fusion.102
  108.4 1.8 fusion.104
  110.2 62.4 %all-gather.9.cloned.1.call-done = f32[16384,128]{1,0:T(8,128)} async-done(((f32[256,128]{1,0:T(8,128)}), f32[16384,128]{1,0:T(8,128)}) %all-gather.9.cloned.1.call-update) | async-done | bytes 8388624 | tf_op jit(solution)/shard_map/all_gather | solution.py:9
  172.6 106.3 %while.32 = (s32[]{:T(128)}, f32[256,128]{1,0:T(8,128)S(1)}, f32[256]{0:T(256)S(1)}, s32[]{:T(128)}, f32[64,256,128]{2,1,0:T(8,128)}, /*index=5*/f32[64,256]{1,0:T(8,128)}, s32[]{:T(128)}, s32[]{:T(128)}) while((s32[]{:T(128)}, f32[256,128]{1,0:T(8,128)S(1)}, f32[256]{0:T(256)S(1)}, s32[]{:T(128)}, f32[64,256,128]{2,1,0:T(8,128)}, ...), condition=%wide.region_15.16_spmd.clone, body=%wide.region_14.15_spmd.clone.sunk | while | flops 99076 | bytes 398459 | solution.py:21
  280.5 2.1 fusion.105
  285.3 1.6 fusion.14
  287.9 1.6 fusion.15
  290.7 80.2 %all-gather.5 = f32[64,1,256]{2,1,0:T(1,128)S(1)} all-gather(f32[1,1,256]{2,1,0:T(1,128)S(1)} %bitcast.225), channel_id=5, replica_groups=mesh['ctx'=64,'head'=8] {'ctx'}, dimensions={0}, use_global_device_ids=true | all-gather | bytes 66560 | tf_op jit(solution)/shard_map/all_gather | solution.py:9
  374.8 1.8 copy.214
  376.6 1.8 copy.215
  381.2 1.6 fusion.6
  385.1 1.5 fusion.44
  387.7 1.5 convolution_add_fusion.2
  389.3 1.4 fusion.4
  390.7 2.0 copy.209
  392.7 1.8 copy.213
  396.7 1.4 convolution_bitcast_fusion.2
  402.3 1.7 fusion.93
  405.1 1.6 fusion.7
  406.8 27.8 %all-gather.11.cloned.1.call-done = f32[16384,128]{1,0:T(8,128)} async-done(((f32[256,128]{1,0:T(8,128)}), f32[16384,128]{1,0:T(8,128)}) %all-gather.11.cloned.1.call-update) | async-done | bytes 8388624 | tf_op jit(solution)/shard_map/all_gather | solution.py:9
  434.6 7.7 rev.6
  442.2 106.4 %while.33 = (s32[]{:T(128)}, f32[256,128]{1,0:T(8,128)S(1)}, f32[256]{0:T(256)S(1)}, s32[]{:T(128)}, f32[64,256,128]{2,1,0:T(8,128)}, /*index=5*/f32[64,256]{1,0:T(8,128)}, s32[]{:T(128)}, s32[]{:T(128)}) while((s32[]{:T(128)}, f32[256,128]{1,0:T(8,128)S(1)}, f32[256]{0:T(256)S(1)}, s32[]{:T(128)}, f32[64,256,128]{2,1,0:T(8,128)}, ...), condition=%wide.region_33.34_spmd.clone, body=%wide.region_32.33_spmd.clone.sunk | while | flops 99076 | bytes 398459 | solution.py:21
  550.8 1.7 convolution_add_fusion.5
  555.7 138.0 %all-reduce.3.cloned.1.call-done = f32[2,128,128]{1,2,0:T(8,128)} async-done(((f32[2,128,128]{1,2,0:T(8,128)}), f32[2,128,128]{1,2,0:T(8,128)}) %all-reduce.3.cloned.1.call-update) | async-done | bytes 131088 | tf_op jit(solution)/shard_map/psum | solution.py:152
  693.8 1.7 copy.181
  695.4 440.1 %all-reduce.5.cloned.1.call-done = f32[128,128]{0,1:T(8,128)} async-done(((f32[128,128]{0,1:T(8,128)}), f32[128,128]{0,1:T(8,128)}) %all-reduce.5.cloned.1.call-update) | async-done | bytes 65552 | tf_op jit(solution)/shard_map/psum | solution.py:153
  1135.6 1.6 copy.182
  1137.1 31.7 %reduce-scatter.5.cloned.1.call-done = f32[64,128]{1,0:T(8,128)} async-done(((f32[512,128]{1,0:T(8,128)}), f32[64,128]{1,0:T(8,128)}) %reduce-scatter.5.cloned.1.call-update) | async-done | bytes 32784 | tf_op jit(solution)/shard_map/reduce_scatter | solution.py:150
  1168.8 40.2 %reduce-scatter.3.cloned.1.call-done = f32[64,128]{1,0:T(8,128)} async-done(((f32[512,128]{1,0:T(8,128)}), f32[64,128]{1,0:T(8,128)}) %reduce-scatter.3.cloned.1.call-update) | async-done | bytes 32784 | tf_op jit(solution)/shard_map/reduce_scatter | solution.py:149
  (489 shorter events, 246.5 us)
Async XLA Ops:
  7.2 2.6 copy-start
  7.2 98.1 %copy-start.12 = (f32[2,128,128]{2,1,0:T(8,128)S(1)}, f32[2,128,128]{2,1,0:T(8,128)}, u32[]{:S(2)}) copy-start(f32[2,128,128]{2,1,0:T(8,128)} %param.18) | copy-start | bytes 393220
  7.2 98.1 %copy-start.4 = (f32[512,256]{1,0:T(8,128)S(1)}, f32[512,256]{1,0:T(8,128)}, u32[]{:S(2)}) copy-start(f32[512,256]{1,0:T(8,128)} %param.12) | copy-start | bytes 1572868
  7.2 165.4 %all-gather.9.cloned.1.call-start = ((), (), s32[]{:S(2)}) async-start(), calls=%async_computation.6 | async-start | bytes 8519680 | tf_op jit(solution)/shard_map/all_gather | solution.py:9
  11.9 422.7 %all-gather.11.cloned.1.call-start = ((), (), s32[]{:S(2)}) async-start(), calls=%async_computation.7 | async-start | bytes 8519680 | tf_op jit(solution)/shard_map/all_gather | solution.py:9
  105.1 174.8 %copy-start.8 = (f32[4,128,128]{1,2,0:T(8,128)S(1)}, f32[4,128,128]{1,2,0:T(8,128)}, u32[]{:S(2)}) copy-start(f32[4,128,128]{1,2,0:T(8,128)} %copy.142) | copy-start | bytes 786436
  105.3 173.6 %copy-start.10 = (f32[128,128]{0,1:T(8,128)}, f32[128,128]{0,1:T(8,128)S(1)}, u32[]{:S(2)}) copy-start(f32[128,128]{0,1:T(8,128)S(1)} %fusion.88) | copy-start | bytes 196612
  279.0 92.5 %copy-start.11 = (f32[128,128]{0,1:T(8,128)S(1)}, f32[128,128]{0,1:T(8,128)}, u32[]{:S(2)}) copy-start(f32[128,128]{0,1:T(8,128)} %copy-done.10) | copy-start | bytes 196612
  282.6 411.2 %all-reduce.3.cloned.1.call-start = ((), (), s32[]{:S(2)}) async-start(), calls=%async_computation.4 | async-start | bytes 262144 | tf_op jit(solution)/shard_map/psum | solution.py:152
  290.6 90.5 %copy-start.15 = (f32[256]{0:T(256)}, f32[256]{0:T(256)S(1)}, u32[]{:S(2)}) copy-start(f32[256]{0:T(256)S(1)} %get-tuple-element.329) | copy-start | bytes 3076
  372.0 0.7 copy-start.6
  379.8 0.7 copy-start.7
  382.8 11.8 copy-start.3
  396.6 3.7 copy-start.1
  406.7 728.8 %all-reduce.5.cloned.1.call-start = ((), (), s32[]{:S(2)}) async-start(), calls=%async_computation.5 | async-start | bytes 131072 | tf_op jit(solution)/shard_map/psum | solution.py:153
  434.6 114.1 %copy-start.5 = (f32[512,256]{0,1:T(8,128)S(1)}, f32[512,256]{0,1:T(8,128)}, u32[]{:S(2)}) copy-start(f32[512,256]{0,1:T(8,128)} %copy.209) | copy-start | bytes 1572868
  434.6 114.9 %copy-start.9 = (f32[512,128]{1,0:T(8,128)S(1)}, f32[512,128]{1,0:T(8,128)}, u32[]{:S(2)}) copy-start(f32[512,128]{1,0:T(8,128)} %param.13) | copy-start | bytes 786436
  434.6 118.0 %copy-start.14 = (f32[128,128]{1,0:T(8,128)S(1)}, f32[128,128]{1,0:T(8,128)}, u32[]{:S(2)}) copy-start(f32[128,128]{1,0:T(8,128)} %param.19) | copy-start | bytes 196612
  442.2 111.6 %copy-start.2 = (f32[512,128]{0,1:T(8,128)S(1)}, f32[512,128]{0,1:T(8,128)}, u32[]{:S(2)}) copy-start(f32[512,128]{0,1:T(8,128)} %copy-done.1) | copy-start | bytes 786436
  442.2 111.6 %copy-start.13 = (f32[2,128,128]{2,1,0:T(8,128)S(1)}, f32[2,128,128]{2,1,0:T(8,128)}, u32[]{:S(2)}) copy-start(f32[2,128,128]{2,1,0:T(8,128)} %param.18) | copy-start | bytes 393220
  550.5 618.3 %reduce-scatter.5.cloned.1.call-start = ((), (), s32[]{:S(2)}) async-start(), calls=%async_computation.3 | async-start | bytes 294912 | tf_op jit(solution)/shard_map/reduce_scatter | solution.py:150
  552.5 656.5 %reduce-scatter.3.cloned.1.call-start = ((), (), s32[]{:S(2)}) async-start(), calls=%async_computation.2 | async-start | bytes 294912 | tf_op jit(solution)/shard_map/reduce_scatter | solution.py:149
Sparse Core Ops, SparseCore 0:
  12.0 160.5 all-gather.8
  282.7 151.7 all-gather.10
  438.0 255.7 all-reduce.2
  699.7 435.8 all-reduce.4
  1139.0 29.7 reduce-scatter.4
  1172.0 36.9 reduce-scatter.2
where the time goes:
time: 1220 us
  waiting for transfers between devices  740 us (61%)
  blocking collectives  168 us (14%)
  other arithmetic  133 us (11%)
  local copies, waits for them, and re-layouts  116 us (10%)
  matrix products  40.1 us (3%)
  between operations  14.6 us (1%)
    psum x1, waiting for transfers between devices, on_device(): grad_kweight = lax.psum(grad_kweight, ('ctx', 'head'))  440 us
    all_gather x2, blocking collectives, entering(): pieces = jax.tree.map(lambda part: lax.all_gather(part, axis), value)  168 us
    psum x1, waiting for transfers between devices, on_device(): grad_qweight = lax.psum(jnp.stack(weight_grads, axis=0), 'ctx')  138 us
    select_n x252, other arithmetic, turn(): jnp.where(position < mine, new, old)  121 us
    all_gather x2, waiting for transfers between devices, entering(): pieces = jax.tree.map(lambda part: lax.all_gather(part, axis), value)  90.2 us
    dynamic_slice x126, local copies, waits for them, and re-layouts, turn(): longer = join(total, jax.tree.map(lambda part: part[position], pieces))  89 us
    reduce_scatter x1, waiting for transfers between devices, on_device(): lax.psum_scatter(grad_key_part, 'head', scatter_dimension=0, tiled=True)  40.2 us
    reduce_scatter x1, waiting for transfers between devices, on_device(): lax.psum_scatter(grad_vals, 'head', scatter_dimension=0, tiled=True)  31.7 us
  transfers between devices with their start and end apart: 6, of which 6 were waited for; matrix products, arithmetic and copies ran while one was open for 14% of the time, Pallas kernels for 0%

commit v1 on v0

--- a/solution.py
+++ b/solution.py
@@ -1,7 +1,17 @@
+import functools
 import jax
 import jax.numpy as jnp
 from jax import lax
 from jax.sharding import PartitionSpec as P
+
+
+def advance_chunk_all(panel, shard_axis, group_axis):
+    for to_i in (shard_axis, group_axis):
+        panel = lax.psum(panel, to_i)
+    return panel
+
+
+switch_the_series = functools.partial(advance_chunk_all, shard_axis="ctx", group_axis="head")
 
 
 def entering(value, axis, join, neutral, backward):
@@ -150,7 +160,7 @@
         lax.psum_scatter(grad_vals, "head", scatter_dimension=0, tiled=True),
     )
     grad_qweight = lax.psum(jnp.stack(weight_grads, axis=0), "ctx")
-    grad_kweight = lax.psum(grad_kweight, ("ctx", "head"))
+    grad_kweight = switch_the_series(grad_kweight)
     return (
         jnp.concatenate(query_grads, axis=1),
         grad_keys,

time: 1220 us -> 976 us (0.80)
  waiting for transfers between devices: 740 us -> 489 us
    psum x1, waiting for transfers between devices: 440 us -> 62.1 us  [advance_chunk_all(): panel = lax.psum(panel, to_i)]
    psum x1, waiting for transfers between devices: 138 us -> 256 us  [on_device(): grad_qweight = lax.psum(jnp.stack(weight_grads, axis=0), 'ctx')]
  transfers between devices with their start and end apart: 6 -> 6, of which waited for: 6 -> 6; matrix products, arithmetic and copies ran while one was open for 14% -> 7% of each run, Pallas kernels for 0% -> 0%
where the time goes in v1:
time: 976 us; the launch traced here: 967 us
  waiting for transfers between devices  489 us (50%)
  blocking collectives  168 us (17%)
  other arithmetic  133 us (14%)
  local copies, waits for them, and re-layouts  116 us (12%)
  matrix products  43.5 us (4%)
  between operations  14.6 us (1%)
    psum x1, waiting for transfers between devices, on_device(): grad_qweight = lax.psum(jnp.stack(weight_grads, axis=0), 'ctx')  256 us
    all_gather x2, blocking collectives, entering(): pieces = jax.tree.map(lambda part: lax.all_gather(part, axis), value)  168 us
    select_n x252, other arithmetic, turn(): jnp.where(position < mine, new, old)  121 us
    all_gather x2, waiting for transfers between devices, entering(): pieces = jax.tree.map(lambda part: lax.all_gather(part, axis), value)  91.4 us
    dynamic_slice x126, local copies, waits for them, and re-layouts, turn(): longer = join(total, jax.tree.map(lambda part: part[position], pieces))  89 us
    psum x1, waiting for transfers between devices, advance_chunk_all(): panel = lax.psum(panel, to_i)  62.1 us
    reduce_scatter x1, waiting for transfers between devices, on_device(): lax.psum_scatter(grad_key_part, 'head', scatter_dimension=0, tiled=True)  40.5 us
    reduce_scatter x1, waiting for transfers between devices, on_device(): lax.psum_scatter(grad_vals, 'head', scatter_dimension=0, tiled=True)  38.8 us
  transfers between devices with their start and end apart: 6, of which 6 were waited for; matrix products, arithmetic and copies ran while one was open for 7% of the time, Pallas kernels for 0%

profile of v1, /device:TPU:2, one launch (start us, length us, event | category | flops | bytes accessed | tf_op | source)
XLA Modules:
  0.0 967.1 jit_solution(702238555240656915)
XLA Ops:
  7.2 1.5 fusion.97
  9.8 2.1 fusion.103
  14.9 87.9 %all-gather.4 = f32[64,1,256]{2,1,0:T(1,128)S(1)} all-gather(f32[1,1,256]{2,1,0:T(1,128)S(1)} %bitcast.226), channel_id=3, replica_groups=mesh['ctx'=64,'head'=8] {'ctx'}, dimensions={0}, use_global_device_ids=true | all-gather | bytes 66560 | tf_op jit(solution)/shard_map/all_gather | solution.py:19
  106.6 1.8 fusion.102
  108.4 1.8 fusion.104
  110.2 62.4 %all-gather.9.cloned.1.call-done = f32[16384,128]{1,0:T(8,128)} async-done(((f32[256,128]{1,0:T(8,128)}), f32[16384,128]{1,0:T(8,128)}) %all-gather.9.cloned.1.call-update) | async-done | bytes 8388624 | tf_op jit(solution)/shard_map/all_gather | solution.py:19
  172.6 106.3 %while.32 = (s32[]{:T(128)}, f32[256,128]{1,0:T(8,128)S(1)}, f32[256]{0:T(256)S(1)}, s32[]{:T(128)}, f32[64,256,128]{2,1,0:T(8,128)}, /*index=5*/f32[64,256]{1,0:T(8,128)}, s32[]{:T(128)}, s32[]{:T(128)}) while((s32[]{:T(128)}, f32[256,128]{1,0:T(8,128)S(1)}, f32[256]{0:T(256)S(1)}, s32[]{:T(128)}, f32[64,256,128]{2,1,0:T(8,128)}, ...), condition=%wide.region_15.16_spmd.clone, body=%wide.region_14.15_spmd.clone.sunk | while | flops 99076 | bytes 398459 | solution.py:31
  280.5 2.1 fusion.105
  285.3 1.6 fusion.14
  287.9 1.6 fusion.15
  290.7 80.0 %all-gather.5 = f32[64,1,256]{2,1,0:T(1,128)S(1)} all-gather(f32[1,1,256]{2,1,0:T(1,128)S(1)} %bitcast.225), channel_id=5, replica_groups=mesh['ctx'=64,'head'=8] {'ctx'}, dimensions={0}, use_global_device_ids=true | all-gather | bytes 66560 | tf_op jit(solution)/shard_map/all_gather | solution.py:19
  374.7 1.8 copy.214
  376.5 1.8 copy.215
  381.0 1.6 fusion.6
  384.9 1.5 fusion.44
  387.6 1.5 convolution_add_fusion.2
  390.6 2.0 copy.209
  392.6 1.8 copy.213
  396.5 1.4 convolution_bitcast_fusion.2
  402.2 2.4 fusion.93
  405.6 28.9 %all-gather.11.cloned.1.call-done = f32[16384,128]{1,0:T(8,128)} async-done(((f32[256,128]{1,0:T(8,128)}), f32[16384,128]{1,0:T(8,128)}) %all-gather.11.cloned.1.call-update) | async-done | bytes 8388624 | tf_op jit(solution)/shard_map/all_gather | solution.py:19
  434.6 7.7 rev.6
  442.2 106.4 %while.33 = (s32[]{:T(128)}, f32[256,128]{1,0:T(8,128)S(1)}, f32[256]{0:T(256)S(1)}, s32[]{:T(128)}, f32[64,256,128]{2,1,0:T(8,128)}, /*index=5*/f32[64,256]{1,0:T(8,128)}, s32[]{:T(128)}, s32[]{:T(128)}) while((s32[]{:T(128)}, f32[256,128]{1,0:T(8,128)S(1)}, f32[256]{0:T(256)S(1)}, s32[]{:T(128)}, f32[64,256,128]{2,1,0:T(8,128)}, ...), condition=%wide.region_33.34_spmd.clone, body=%wide.region_32.33_spmd.clone.sunk | while | flops 99076 | bytes 398459 | solution.py:31
  550.5 1.7 fusion.7
  552.2 255.8 %all-reduce.6.cloned.1.call-done = (f32[2,128,128]{1,2,0:T(8,128)}, f32[128,128]{0,1:T(8,128)}) async-done(((f32[2,128,128]{1,2,0:T(8,128)}, f32[128,128]{0,1:T(8,128)}), (f32[2,128,128]{1,2,0:T(8,128)}, f32[128,128]{0,1:T(8,128)})) %all-reduce.6.cloned.1.call-update) | async-done | bytes 196624 | tf_op jit(solution)/shard_map/psum | solution.py:162
  808.3 1.7 convolution_add_fusion.5
  810.0 2.1 fusion.106
  815.7 1.7 copy.181
  817.4 62.1 %all-reduce.4.cloned.1.call-done = f32[128,128]{0,1:T(8,128)} async-done(((f32[128,128]{0,1:T(8,128)}), f32[128,128]{0,1:T(8,128)}) %all-reduce.4.cloned.1.call-update) | async-done | bytes 65552 | tf_op jit(solution)/shard_map/psum | solution.py:10
  879.4 1.6 copy.182
  881.0 38.8 %reduce-scatter.5.cloned.1.call-done = f32[64,128]{1,0:T(8,128)} async-done(((f32[512,128]{1,0:T(8,128)}), f32[64,128]{1,0:T(8,128)}) %reduce-scatter.5.cloned.1.call-update) | async-done | bytes 32784 | tf_op jit(solution)/shard_map/reduce_scatter | solution.py:160
  919.8 40.5 %reduce-scatter.3.cloned.1.call-done = f32[64,128]{1,0:T(8,128)} async-done(((f32[512,128]{1,0:T(8,128)}), f32[64,128]{1,0:T(8,128)}) %reduce-scatter.3.cloned.1.call-update) | async-done | bytes 32784 | tf_op jit(solution)/shard_map/reduce_scatter | solution.py:159
  (485 shorter events, 248.3 us)
Async XLA Ops:
  7.2 2.6 copy-start
  7.2 98.1 %copy-start.12 = (f32[2,128,128]{2,1,0:T(8,128)S(1)}, f32[2,128,128]{2,1,0:T(8,128)}, u32[]{:S(2)}) copy-start(f32[2,128,128]{2,1,0:T(8,128)} %param.18) | copy-start | bytes 393220
  7.2 98.1 %copy-start.4 = (f32[512,256]{1,0:T(8,128)S(1)}, f32[512,256]{1,0:T(8,128)}, u32[]{:S(2)}) copy-start(f32[512,256]{1,0:T(8,128)} %param.12) | copy-start | bytes 1572868
  7.2 165.4 %all-gather.9.cloned.1.call-start = ((), (), s32[]{:S(2)}) async-start(), calls=%async_computation.5 | async-start | bytes 8519680 | tf_op jit(solution)/shard_map/all_gather | solution.py:19
  11.9 422.7 %all-gather.11.cloned.1.call-start = ((), (), s32[]{:S(2)}) async-start(), calls=%async_computation.6 | async-start | bytes 8519680 | tf_op jit(solution)/shard_map/all_gather | solution.py:19
  105.1 174.8 %copy-start.8 = (f32[4,128,128]{1,2,0:T(8,128)S(1)}, f32[4,128,128]{1,2,0:T(8,128)}, u32[]{:S(2)}) copy-start(f32[4,128,128]{1,2,0:T(8,128)} %copy.142) | copy-start | bytes 786436
  105.3 173.6 %copy-start.10 = (f32[128,128]{0,1:T(8,128)}, f32[128,128]{0,1:T(8,128)S(1)}, u32[]{:S(2)}) copy-start(f32[128,128]{0,1:T(8,128)S(1)} %fusion.88) | copy-start | bytes 196612
  279.0 92.4 %copy-start.11 = (f32[128,128]{0,1:T(8,128)S(1)}, f32[128,128]{0,1:T(8,128)}, u32[]{:S(2)}) copy-start(f32[128,128]{0,1:T(8,128)} %copy-done.10) | copy-start | bytes 196612
  282.6 525.3 %all-reduce.6.cloned.1.call-start = ((), (), s32[]{:S(2)}) async-start(), calls=%async_computation.7 | async-start | bytes 393216 | tf_op jit(solution)/shard_map/psum | solution.py:162
  290.7 90.4 %copy-start.13 = (f32[256]{0:T(256)}, f32[256]{0:T(256)S(1)}, u32[]{:S(2)}) copy-start(f32[256]{0:T(256)S(1)} %get-tuple-element.331) | copy-start | bytes 3076
  371.8 0.7 copy-start.6
  379.6 0.7 copy-start.7
  382.6 11.7 %copy-start.3 = (f32[512,128]{0,1:T(8,128)S(1)}, f32[512,128]{0,1:T(8,128)}, u32[]{:S(2)}) copy-start(f32[512,128]{0,1:T(8,128)} %copy.214) | copy-start | bytes 786436
  396.5 3.7 copy-start.1
  434.6 114.0 %copy-start.5 = (f32[512,256]{0,1:T(8,128)S(1)}, f32[512,256]{0,1:T(8,128)}, u32[]{:S(2)}) copy-start(f32[512,256]{0,1:T(8,128)} %copy.209) | copy-start | bytes 1572868
  434.6 114.8 %copy-start.9 = (f32[512,128]{1,0:T(8,128)S(1)}, f32[512,128]{1,0:T(8,128)}, u32[]{:S(2)}) copy-start(f32[512,128]{1,0:T(8,128)} %param.13) | copy-start | bytes 786436
  442.2 369.9 %copy-start.2 = (f32[512,128]{0,1:T(8,128)S(1)}, f32[512,128]{0,1:T(8,128)}, u32[]{:S(2)}) copy-start(f32[512,128]{0,1:T(8,128)} %copy-done.1) | copy-start | bytes 786436
  550.5 329.0 %all-reduce.4.cloned.1.call-start = ((), (), s32[]{:S(2)}) async-start(), calls=%async_computation.4 | async-start | bytes 131072 | tf_op jit(solution)/shard_map/psum | solution.py:10
  808.0 111.8 %reduce-scatter.5.cloned.1.call-start = ((), (), s32[]{:S(2)}) async-start(), calls=%async_computation.3 | async-start | bytes 294912 | tf_op jit(solution)/shard_map/reduce_scatter | solution.py:160
  810.0 150.3 %reduce-scatter.3.cloned.1.call-start = ((), (), s32[]{:S(2)}) async-start(), calls=%async_computation.2 | async-start | bytes 294912 | tf_op jit(solution)/shard_map/reduce_scatter | solution.py:159
Sparse Core Ops, SparseCore 0:
  12.0 160.5 all-gather.8
  282.8 151.7 all-gather.10
  550.6 257.3 all-reduce.5
  810.2 69.1 all-reduce.3
  882.6 37.1 reduce-scatter.4
  923.3 36.9 reduce-scatter.2
